TPU v7x, 128 devices: a whole 4x4x4 slice. The times are simulated.
128 devices in a mesh: section: 2 (over y_lo), shard: 2 (over y_hi), rep: 32 (over z, x, core).
Axes of the slice: x: 4, y: 4 (y_hi: 2, y_lo: 2; y = y_hi * 2 + y_lo), z: 4, core: 2. Of those that a mesh axis runs over, the one named last changes fastest.
Arguments:
- tokens: bfloat16 [14336, 960], P(('shard', 'rep')), may hold values from -6 to 6
- segments: int32 [128, 112], P(('shard', 'rep')), may hold values from 0 to 2, as said below
- cotangent: float32 [14336, 960], P(('shard', 'rep')), may hold values from -6 to 6
- qkv_weight: bfloat16 [2, 960, 1600], P('section', 'shard'), may hold values from -0.1875 to 0.1875
- output_weight: bfloat16 [2, 960, 960], P('section', 'shard'), may hold values from -0.75 to 0.75
- gateup_weight: bfloat16 [2, 960, 5120], P('section', 'shard'), may hold values from -0.1875 to 0.1875
- down_weight: bfloat16 [2, 2560, 960], P('section', 'shard'), may hold values from -0.125 to 0.125
- norm_gains: bfloat16 [2, 2, 960], P('section', None, 'shard'), may hold values from 0.099609375 to 1.8984375
Outputs:
- activations: float32 [2, 14336, 960], P('section', ('shard', 'rep'))
- input_grads: float32 [2, 14336, 960], P('section', ('shard', 'rep'))
- qkv_grad: float32 [2, 960, 1600], P('section', ('shard', 'rep'))
- output_grad: float32 [2, 960, 960], P('section', ('shard', 'rep'))
- gateup_grad: float32 [2, 960, 5120], P('section', ('shard', 'rep'))
- down_grad: float32 [2, 2560, 960], P('section', ('shard', 'rep'))
- gains_grad: float32 [2, 2, 960], P('section', None, ('shard', 'rep'))
Inputs may be any that keep to these rules, and one draw needn't show every extreme that they name: `segments`: within each row, numbers never fall and each of the 3 numbers covers at least one position; in every row exactly one number covers 84 positions, and the other two share the remaining 112 - 84 positions.
All inputs are finite; a program needn't handle non-finite values.
Results may differ from a plain program's by a relative error of at most 0.03.
Values may be sent and summed in bfloat16 or wider, within the bound.
No kernel may reach another device: no remote copies, remote signals or barrier semaphores. Data moves between devices by JAX's collectives and lax.ppermute only.
A program may use at most 256 MiB of HBM per device.

v0:
```python
import jax
import jax.numpy as jnp
from jax import lax
from jax.sharding import PartitionSpec as P

HEADS = 15
KV_HEADS = 5
HEAD = 64
FF = 2560


EPSILON = 1e-05
ROPE_BASE = 100000.0
NEGATIVE = -1e30


def sent_together(arrays, axis, dim, along):
    both = jnp.concatenate(arrays, axis=along)
    result, at, outs = (lax.all_gather(both, axis, axis=dim, tiled=True), 0, [])
    for a in arrays:
        outs.append(lax.slice_in_dim(result, at, at + a.shape[along], axis=along))
        at += a.shape[along]
    return tuple(outs)


def from_behind(shard, axis, by):
    size = lax.axis_size(axis)
    pairs = [(i, i + by) for i in range(size) if 0 <= i + by < size]
    return lax.ppermute(shard, axis, pairs)


def side_by_side(arrays, axis, dim, along):
    both = jnp.concatenate(arrays, axis=along)
    result, at, outs = (lax.psum_scatter(both, axis, scatter_dimension=dim, tiled=True), 0, [])
    for a in arrays:
        outs.append(lax.slice_in_dim(result, at, at + a.shape[along], axis=along))
        at += a.shape[along]
    return tuple(outs)


def positions(labels):
    row_count = labels.shape[0]
    earlier = jnp.sum((labels[None, :] < labels[:, None]).astype(jnp.int32), axis=1)
    return (jnp.arange(row_count, dtype=jnp.int32) - earlier).astype(jnp.float32)


def tables(labels):
    half_width = HEAD // 2
    frequency = ROPE_BASE ** (-jnp.arange(half_width, dtype=jnp.float32) * 2.0 / HEAD)
    angles = positions(labels)[:, None] * frequency[None, :]
    return (jnp.cos(angles)[:, None, :], jnp.sin(angles)[:, None, :])


def rotate(values, cosine_table, sine_table):
    half_width = values.shape[-1] // 2
    first_half = values[..., :half_width]
    second_half = values[..., half_width:]
    return jnp.concatenate(
        [
            first_half * cosine_table - second_half * sine_table,
            second_half * cosine_table + first_half * sine_table,
        ],
        axis=-1,
    )


def unrotate(grads_in, cosine_table, sine_table):
    half_width = grads_in.shape[-1] // 2
    first_half = grads_in[..., :half_width]
    second_half = grads_in[..., half_width:]
    return jnp.concatenate(
        [
            first_half * cosine_table + second_half * sine_table,
            second_half * cosine_table - first_half * sine_table,
        ],
        axis=-1,
    )


def visible(labels):
    row_count = labels.shape[0]
    row_order = jnp.arange(row_count, dtype=jnp.int32)
    return (labels[:, None] == labels[None, :]) & (row_order[None, :] <= row_order[:, None])


def forward(stream, labels, weights):
    qkv_full, out_full, gateup_full, down_full, gain_full = weights
    row_count = stream.shape[0]
    group_size = HEADS // KV_HEADS
    query_width = HEADS * HEAD
    key_width = KV_HEADS * HEAD
    head_scale = HEAD ** (-0.5)
    first_gain = gain_full[0].astype(jnp.float32)
    second_gain = gain_full[1].astype(jnp.float32)
    first_scale = lax.rsqrt(jnp.mean(stream * stream, axis=-1, keepdims=True) + EPSILON)
    first_normed = stream * first_scale
    attn_norm = (first_normed * first_gain).astype(jnp.bfloat16)
    projected = jnp.dot(attn_norm, qkv_full, preferred_element_type=jnp.float32)
    cosine_table, sine_table = tables(labels)
    query_heads = rotate(
        projected[:, :query_width].reshape(row_count, HEADS, HEAD), cosine_table, sine_table
    )
    query_heads = query_heads.astype(jnp.bfloat16).reshape(row_count, KV_HEADS, group_size, HEAD)
    key_heads = rotate(
        projected[:, query_width : query_width + key_width].reshape(row_count, KV_HEADS, HEAD),
        cosine_table,
        sine_table,
    )
    key_heads = key_heads.astype(jnp.bfloat16)
    value_heads = (
        projected[:, query_width + key_width :]
        .reshape(row_count, KV_HEADS, HEAD)
        .astype(jnp.bfloat16)
    )
    scores = (
        jnp.einsum("qkge,ske->kgqs", query_heads, key_heads, preferred_element_type=jnp.float32)
        * head_scale
    )
    masked = jnp.where(visible(labels)[None, None], scores, NEGATIVE)
    maximum = jnp.max(masked, axis=-1, keepdims=True)
    exponent = jnp.exp(masked - maximum)
    probability = exponent / jnp.sum(exponent, axis=-1, keepdims=True)
    prob_low = probability.astype(jnp.bfloat16)
    mixed_heads = jnp.einsum(
        "kgqs,ske->qkge", prob_low, value_heads, preferred_element_type=jnp.float32
    )
    mixed_heads = mixed_heads.reshape(row_count, query_width).astype(jnp.bfloat16)
    middle = stream + jnp.dot(mixed_heads, out_full, preferred_element_type=jnp.float32)
    second_scale = lax.rsqrt(jnp.mean(middle * middle, axis=-1, keepdims=True) + EPSILON)
    second_normed = middle * second_scale
    ffn_norm = (second_normed * second_gain).astype(jnp.bfloat16)
    gateup = jnp.dot(ffn_norm, gateup_full, preferred_element_type=jnp.float32)
    gate_part = gateup[:, :FF]
    upward = gateup[:, FF:]
    hidden = (gate_part * jax.nn.sigmoid(gate_part) * upward).astype(jnp.bfloat16)
    output = middle + jnp.dot(hidden, down_full, preferred_element_type=jnp.float32)
    stored = (
        first_gain,
        second_gain,
        first_scale,
        first_normed,
        attn_norm,
        cosine_table,
        sine_table,
        query_heads,
        key_heads,
        value_heads,
        probability,
        prob_low,
        mixed_heads,
        second_scale,
        second_normed,
        ffn_norm,
        gate_part,
        upward,
        hidden,
    )
    return (output, stored)


def norm_back(incoming, gain_row, scale_col, normed):
    scaled = incoming * gain_row
    return scale_col * (scaled - normed * jnp.mean(scaled * normed, axis=-1, keepdims=True))


def backward(upstream, stream, labels, weights):
    qkv_full, out_full, gateup_full, down_full, gain_full = weights
    recomputed, stored = forward(stream, labels, weights)
    (
        first_gain,
        second_gain,
        first_scale,
        first_normed,
        attn_norm,
        cosine_table,
        sine_table,
        query_heads,
        key_heads,
        value_heads,
        probability,
        prob_low,
        mixed_heads,
        second_scale,
        second_normed,
        ffn_norm,
        gate_part,
        upward,
        hidden,
    ) = stored
    row_count = stream.shape[0]
    group_size = HEADS // KV_HEADS
    head_scale = HEAD ** (-0.5)
    down_in = upstream.astype(jnp.bfloat16)
    down_grad = jnp.dot(hidden.T, down_in, preferred_element_type=jnp.float32)
    hidden_grad = jnp.dot(down_in, down_full.T, preferred_element_type=jnp.float32)
    sigmoid_gate = jax.nn.sigmoid(gate_part)
    gate_grad = hidden_grad * upward * sigmoid_gate * (1.0 + gate_part * (1.0 - sigmoid_gate))
    upward_grad = hidden_grad * gate_part * sigmoid_gate
    gateup_in = jnp.concatenate([gate_grad, upward_grad], axis=1).astype(jnp.bfloat16)
    gateup_grad = jnp.dot(ffn_norm.T, gateup_in, preferred_element_type=jnp.float32)
    second_incoming = jnp.dot(gateup_in, gateup_full.T, preferred_element_type=jnp.float32)
    second_gain_grad = jnp.sum(second_incoming * second_normed, axis=0)
    middle_grad = upstream + norm_back(second_incoming, second_gain, second_scale, second_normed)
    branch_in = middle_grad.astype(jnp.bfloat16)
    output_grad = jnp.dot(mixed_heads.T, branch_in, preferred_element_type=jnp.float32)
    mixed_grad = jnp.dot(branch_in, out_full.T, preferred_element_type=jnp.float32).astype(
        jnp.bfloat16
    )
    mixed_grad = mixed_grad.reshape(row_count, KV_HEADS, group_size, HEAD)
    prob_grad = jnp.einsum(
        "qkge,ske->kgqs", mixed_grad, value_heads, preferred_element_type=jnp.float32
    )
    value_grad = jnp.einsum(
        "kgqs,qkge->ske", prob_low, mixed_grad, preferred_element_type=jnp.float32
    )
    score_grad = probability * (
        prob_grad - jnp.sum(prob_grad * probability, axis=-1, keepdims=True)
    )
    score_grad = score_grad.astype(jnp.bfloat16)
    query_grad = (
        jnp.einsum("kgqs,ske->qkge", score_grad, key_heads, preferred_element_type=jnp.float32)
        * head_scale
    )
    key_grad = (
        jnp.einsum("kgqs,qkge->ske", score_grad, query_heads, preferred_element_type=jnp.float32)
        * head_scale
    )
    query_grad = unrotate(query_grad.reshape(row_count, HEADS, HEAD), cosine_table, sine_table)
    key_grad = unrotate(key_grad, cosine_table, sine_table)
    projected_in = jnp.concatenate(
        [
            query_grad.reshape(row_count, HEADS * HEAD),
            key_grad.reshape(row_count, KV_HEADS * HEAD),
            value_grad.reshape(row_count, KV_HEADS * HEAD),
        ],
        axis=1,
    ).astype(jnp.bfloat16)
    qkv_grad = jnp.dot(attn_norm.T, projected_in, preferred_element_type=jnp.float32)
    first_incoming = jnp.dot(projected_in, qkv_full.T, preferred_element_type=jnp.float32)
    first_gain_grad = jnp.sum(first_incoming * first_normed, axis=0)
    stream_grad = middle_grad + norm_back(first_incoming, first_gain, first_scale, first_normed)
    gain_grads = jnp.stack([first_gain_grad, second_gain_grad])
    return (stream_grad, (qkv_grad, output_grad, gateup_grad, down_grad, gain_grads))


def shards(
    tokens, segments, cotangent, qkv_weight, output_weight, gateup_weight, down_weight, norm_gains
):
    leading = lax.axis_index("section") == 0
    micro_count = segments.shape[0]
    block_rows = segments.shape[1]
    inputs = tokens.astype(jnp.float32).reshape(micro_count, block_rows, -1)
    pulled = cotangent.reshape(micro_count, block_rows, -1)

    def fetch_weights():
        gathered = (
            *sent_together((qkv_weight, output_weight, gateup_weight), "shard", 1, 2),
            lax.all_gather(down_weight, "shard", axis=1, tiled=True),
            lax.all_gather(norm_gains, "shard", axis=2, tiled=True),
        )
        return tuple((piece[0] for piece in gathered))

    section_inputs = []
    section_outputs = []
    previous = None
    for moment in range(micro_count + 1):
        own_index = min(moment, micro_count - 1)
        back_index = max(moment - 1, 0)
        if moment == 0:
            arrived = jnp.zeros_like(inputs[0])
        else:
            arrived = from_behind(previous, "section", 1)
        stream = jnp.where(leading, inputs[own_index], arrived)
        labels = jnp.where(leading, segments[own_index], segments[back_index])
        weights = fetch_weights()
        result, stored = forward(stream, labels, weights)
        section_inputs.append(stream)
        section_outputs.append(result)
        previous = result
    kept_inputs = [
        jnp.where(leading, section_inputs[index], section_inputs[index + 1])
        for index in range(micro_count)
    ]
    kept_outputs = [
        jnp.where(leading, section_outputs[index], section_outputs[index + 1])
        for index in range(micro_count)
    ]
    activations = jnp.concatenate(kept_outputs, axis=0)[None]
    totals = None
    tick_grads = []
    previous = None
    for moment in range(micro_count + 1):
        late_index = min(moment, micro_count - 1)
        early_index = max(moment - 1, 0)
        if moment == 0:
            arrived = jnp.zeros_like(inputs[0])
        else:
            arrived = from_behind(previous, "section", -1)
        active = jnp.where(leading, moment >= 1, moment < micro_count).astype(jnp.float32)
        upstream = jnp.where(leading, arrived, pulled[late_index]) * active
        stream = jnp.where(leading, kept_inputs[early_index], kept_inputs[late_index])
        labels = jnp.where(leading, segments[early_index], segments[late_index])
        weights = fetch_weights()
        downstream, grad_terms = backward(upstream, stream, labels, weights)
        if totals is None:
            totals = grad_terms
        else:
            totals = tuple((total + term for total, term in zip(totals, grad_terms)))
        tick_grads.append(downstream)
        previous = downstream
    input_list = [
        jnp.where(leading, tick_grads[index + 1], tick_grads[index]) for index in range(micro_count)
    ]
    input_grads = jnp.concatenate(input_list, axis=0)[None]
    leading_totals = tuple((total[None] for total in totals))
    halves = (
        *tuple(
            (
                part.astype(jnp.float32)
                for part in side_by_side(
                    (
                        leading_totals[0].astype(jnp.bfloat16),
                        leading_totals[1].astype(jnp.bfloat16),
                        leading_totals[2].astype(jnp.bfloat16),
                    ),
                    "shard",
                    1,
                    2,
                )
            )
        ),
        lax.psum_scatter(
            leading_totals[3].astype(jnp.bfloat16), "shard", scatter_dimension=1, tiled=True
        ).astype(jnp.float32),
        lax.psum_scatter(
            leading_totals[4].astype(jnp.bfloat16), "shard", scatter_dimension=2, tiled=True
        ).astype(jnp.float32),
    )
    owned = (
        lax.psum_scatter(
            halves[0].astype(jnp.bfloat16), "rep", scatter_dimension=1, tiled=True
        ).astype(jnp.float32),
        lax.psum_scatter(
            halves[1].astype(jnp.bfloat16), "rep", scatter_dimension=1, tiled=True
        ).astype(jnp.float32),
        lax.psum_scatter(
            halves[2].astype(jnp.bfloat16), "rep", scatter_dimension=1, tiled=True
        ).astype(jnp.float32),
        lax.psum_scatter(
            halves[3].astype(jnp.bfloat16), "rep", scatter_dimension=1, tiled=True
        ).astype(jnp.float32),
        lax.psum_scatter(
            halves[4].astype(jnp.bfloat16), "rep", scatter_dimension=2, tiled=True
        ).astype(jnp.float32),
    )
    return (activations, input_grads, owned[0], owned[1], owned[2], owned[3], owned[4])


def solution(mesh):
    in_specs = (
        P(("shard", "rep"), None),
        P(("shard", "rep"), None),
        P(("shard", "rep"), None),
        P("section", "shard", None),
        P("section", "shard", None),
        P("section", "shard", None),
        P("section", "shard", None),
        P("section", None, "shard"),
    )
    out_specs = (
        P("section", ("shard", "rep"), None),
        P("section", ("shard", "rep"), None),
        P("section", ("shard", "rep"), None),
        P("section", ("shard", "rep"), None),
        P("section", ("shard", "rep"), None),
        P("section", ("shard", "rep"), None),
        P("section", None, ("shard", "rep")),
    )
    return jax.shard_map(shards, mesh=mesh, in_specs=in_specs, out_specs=out_specs, check_vma=False)
```

profile of v0, /device:TPU:2, one launch (start us, length us, event | category | flops | bytes accessed | tf_op | source)
XLA Modules:
  0.0 893.5 jit_solution(12244830983397827961)
XLA Ops:
  7.2 11.8 %concatenate.164 = bf16[1,480,7680]{2,1,0:T(8,128)(2,1)} concatenate(bf16[1,480,1600]{2,1,0:T(8,128)(2,1)} %param.11, bf16[1,480,960]{2,1,0:T(8,128)(2,1)} %param.12, bf16[1,480,5120]{2,1,0:T(8,128)(2,1)} %param.13), dimensions={2} | concatenate | bytes 14745600 | tf_op jit(solution)/shard_map/concatenate | solution.py:18
  20.2 9.9 %all_gather.6 = bf16[1,2,960]{1,0,2:T(2,128)(2,1)S(1)} all-gather(bf16[1,2,480]{1,0,2:T(2,128)(2,1)S(1)} %copy.165), channel_id=1, replica_groups=mesh['section'=2,'shard'=2,'rep'=32] {'shard'}, dimensions={2}, use_global_device_ids=true | all-gather | bytes 5760 | tf_op jit(solution)/shard_map/all_gather | solution.py:259
  32.2 5.9 fusion.95
  38.1 163.8 %all-gather.3.cloned.1.call-done = bf16[1,960,7680]{2,1,0:T(8,128)(2,1)} async-done(((bf16[1,480,7680]{2,1,0:T(8,128)(2,1)}), bf16[1,960,7680]{2,1,0:T(8,128)(2,1)}) %all-gather.3.cloned.1.call-update) | async-done | bytes 14745616 | tf_op jit(solution)/shard_map/all_gather | solution.py:19
  209.8 7.6 fusion.94
  217.4 54.4 %all-gather.5.cloned.1.call-done = bf16[1,2560,960]{1,2,0:T(8,128)(2,1)} async-done(((bf16[1,1280,960]{1,2,0:T(8,128)(2,1)}), bf16[1,2560,960]{1,2,0:T(8,128)(2,1)}) %all-gather.5.cloned.1.call-update) | async-done | bytes 4915216 | tf_op jit(solution)/shard_map/all_gather | solution.py:258
  271.9 4.7 fusion.49
  279.4 9.5 %collective-permute-done = f32[112,960]{1,0:T(8,128)S(1)} collective-permute-done((f32[112,960]{1,0:T(8,128)S(1)}, f32[112,960]{1,0:T(8,128)S(1)}, u32[]{:S(2)}, u32[]{:S(2)}) %collective-permute-start) | collective-permute-done | bytes 430112 | tf_op jit(solution)/shard_map/ppermute | solution.py:29
  297.1 5.4 fusion.93
  310.2 8.1 collective-permute-done.1
  338.7 5.5 fusion.91
  371.7 11.6 %subtract_convert_fusion.3 = (bf16[112,15,32]{0,2,1:T(8,128)(2,1)S(1)}, bf16[112,15,32]{0,2,1:T(8,128)(2,1)S(1)}) fusion(f32[112,15,64]{0,2,1:T(8,128)S(1)} %bitcast.517, f32[112,32]{0,1:T(8,128)S(1)} %copy-done.82, f32[112,32]{0,1:T(8,128)S(1)} %copy-done.81), kind=kLoop, calls=%fused_computation.234 | loop fusion | flops 430080 | bytes 673792 | tf_op jit(solution)/shard_map/convert.38
  398.8 6.9 fusion.89
  408.3 5.3 fusion.78
  415.8 5.0 multiply_reduce_fusion.5
  437.3 5.1 fusion.79
  442.5 5.6 collective-permute-done.3
  449.7 6.3 fusion.22
  473.3 8.3 fusion.76
  488.1 11.3 %fusion.74 = f32[960,5120]{1,0:T(8,128)} fusion(bf16[112,2560]{1,0:T(8,128)(2,1)S(1)} %copy-done.59, bf16[112,2560]{1,0:T(8,128)(2,1)S(1)} %copy-done.58, f32[112,960]{1,0:T(8,128)S(1)} %get-tuple-element.148, f32[112]{0:T(128)S(1)} %add_rsqrt_fusion.2, f32[960]{0:T(1024)S(1)} %get-tuple-element.47), kind=kOutput, calls=%fused_computation.132 | convolution fusion | flops 1103621120 | bytes 21242048 | tf_op jit(solution)/shard_map/dot_general | solution.py:200
  517.6 6.0 fusion.23
  523.6 18.3 %fusion.9 = bf16[1,960,5120]{2,1,0:T(8,128)(2,1)} fusion(f32[960,5120]{1,0:T(8,128)} %fusion.76, f32[960,5120]{1,0:T(8,128)} %fusion.74, bf16[112,2560]{1,0:T(8,128)(2,1)} %copy-done.50, bf16[112,2560]{1,0:T(8,128)(2,1)} %copy-done.49, f32[112,960]{1,0:T(8,128)} %copy-done.3, f32[112]{0:T(128)S(1)} %copy-done.143, f32[960]{0:T(1024)S(1)} %get-tuple-element.47), kind=kOutput, calls=%fused_computation.9 | convolution fusion | flops 1118366720 | bytes 50733248 | tf_op jit(solution)/shard_map/dot_general | solution.py:200
  541.9 5.4 fusion.24
  547.3 21.3 %concatenate.203 = bf16[1,960,7680]{2,1,0:T(8,128)(2,1)} concatenate(bf16[1,960,1600]{2,1,0:T(8,128)(2,1)S(1)} %fusion.23, bf16[1,960,960]{2,1,0:T(8,128)(2,1)} %fusion.24, bf16[1,960,5120]{2,1,0:T(8,128)(2,1)} %fusion.9), dimensions={2} | concatenate | bytes 29491200 | tf_op jit(solution)/shard_map/concatenate | solution.py:33
  577.6 6.4 fusion.92
  585.7 11.6 %copy.202 = bf16[1,1280,960]{2,0,1:T(2,128)(2,1)} copy(bf16[1,1280,960]{1,2,0:T(8,128)(2,1)} %reduce-scatter.18.cloned.1.call-done) | data formatting | bytes 4915200 | tf_op jit(solution)/shard_map/reduce_scatter | solution.py:332
  601.4 59.6 %all-reduce.4 = bf16[1,2,480]{2,1,0:T(2,128)(2,1)S(1)} all-reduce(bf16[1,2,480]{2,1,0:T(2,128)(2,1)S(1)} %copy.247), channel_id=9, replica_groups=mesh['section'=2,'shard'=2,'rep'=32] {'rep'}, use_global_device_ids=true, to_apply=%region_50.51.clone | all-reduce | flops 960 | bytes 3840
  661.6 79.6 %reduce-scatter.16.cloned.1.call-done = bf16[1,480,7680]{2,1,0:T(8,128)(2,1)} async-done(((bf16[1,960,7680]{2,1,0:T(8,128)(2,1)}), bf16[1,480,7680]{2,1,0:T(8,128)(2,1)}) %reduce-scatter.16.cloned.1.call-update) | async-done | bytes 7372816 | tf_op jit(solution)/shard_map/reduce_scatter | solution.py:34
  743.0 5.0 slice.444
  748.0 79.7 %fusion.229 = (bf16[16,1600]{1,0:T(8,128)(2,1)S(1)}, bf16[16,960]{1,0:T(8,128)(2,1)S(1)}, bf16[16,5120]{1,0:T(8,128)(2,1)S(1)}) fusion(bf16[1,480,1600]{2,1,0:T(8,128)(2,1)S(1)} %slice-done.15, bf16[1,480,960]{2,1,0:T(8,128)(2,1)S(1)} %slice.443, bf16[1,480,5120]{2,1,0:T(8,128)(2,1)} %slice.444), kind=kCustom, calls=%all-reduce-scatter.3 | all-reduce-scatter fusion | flops 3932161 | bytes 7619072
  831.6 33.3 %all-reduce.11.cloned.1.call-done = bf16[1,1280,960]{2,0,1:T(2,128)(2,1)} async-done(((bf16[1,1280,960]{2,0,1:T(2,128)(2,1)}), bf16[1,1280,960]{2,0,1:T(2,128)(2,1)}) %all-reduce.11.cloned.1.call-update) | async-done | bytes 2457616
  872.2 4.6 collective-permute-start.5
  (603 shorter events, 191.3 us)
Async XLA Ops:
  7.2 194.7 %all-gather.3.cloned.1.call-start = ((), (), s32[]{:S(2)}) async-start(), calls=%async_computation.3 | async-start | bytes 22118400 | tf_op jit(solution)/shard_map/all_gather | solution.py:19
  19.1 252.8 %all-gather.5.cloned.1.call-start = ((), (), s32[]{:S(2)}) async-start(), calls=%async_computation.4 | async-start | bytes 7372800 | tf_op jit(solution)/shard_map/all_gather | solution.py:258
  19.8 565.9 %reduce-scatter.18.cloned.1.call-start = ((), (), s32[]{:S(2)}) async-start(), calls=%async_computation.6 | async-start | bytes 7372800 | tf_op jit(solution)/shard_map/reduce_scatter | solution.py:332
  19.9 184.5 %copy-start.136 = (s32[112]{0:T(128)}, s32[112]{0:T(128)S(1)}, u32[]{:S(2)}) copy-start(s32[112]{0:T(128)S(1)} %get-tuple-element.117) | copy-start | bytes 1348
  20.0 184.5 %copy-start.124 = (s32[112]{0:T(128)}, s32[112]{0:T(128)S(1)}, u32[]{:S(2)}) copy-start(s32[112]{0:T(128)S(1)} %get-tuple-element.114) | copy-start | bytes 1348
  20.0 184.5 %copy-start.138 = (s32[112]{0:T(128)}, s32[112]{0:T(128)S(1)}, u32[]{:S(2)}) copy-start(s32[112]{0:T(128)S(1)} %get-tuple-element.113) | copy-start | bytes 1348
  31.3 174.0 %copy-start.119 = (pred[112,112]{0,1:T(8,128)(4,1)}, pred[112,112]{0,1:T(8,128)(4,1)S(1)}, u32[]{:S(2)}) copy-start(pred[112,112]{0,1:T(8,128)(4,1)S(1)} %get-tuple-element.172) | copy-start | bytes 37636
  32.2 301.4 %copy-start.43 = (f32[112,32]{0,1:T(8,128)}, f32[112,32]{0,1:T(8,128)S(1)}, u32[]{:S(2)}) copy-start(f32[112,32]{0,1:T(8,128)S(1)} %get-tuple-element.132) | copy-start | bytes 43012
  276.6 12.3 %collective-permute-start = (f32[112,960]{1,0:T(8,128)S(1)}, f32[112,960]{1,0:T(8,128)S(1)}, u32[]{:S(2)}, u32[]{:S(2)}) collective-permute-start(f32[112,960]{1,0:T(8,128)S(1)} %fusion.49), channel_id=1, source_target_pairs={{0,64},{1,65},{2,66},{3,67},{4,68},{5,69},{6,70},{7,71},{8,72},{9,... | collective-permute-start | bytes 1290248 | tf_op jit(solution)/shard_map/ppermute | solution.py:29
  305.0 14.5 %copy-start.155 = (f32[112,960]{1,0:T(8,128)}, f32[112,960]{1,0:T(8,128)S(1)}, u32[]{:S(2)}) copy-start(f32[112,960]{1,0:T(8,128)S(1)} %get-tuple-element.163) | copy-start | bytes 1290244
  305.0 13.3 %collective-permute-start.1 = (f32[112,960]{1,0:T(8,128)S(1)}, f32[112,960]{1,0:T(8,128)S(1)}, u32[]{:S(2)}, u32[]{:S(2)}) collective-permute-start(f32[112,960]{1,0:T(8,128)S(1)} %get-tuple-element.163), channel_id=1, source_target_pairs={{0,64},{1,65},{2,66},{3,67},{4,68},{5,69},{6,70},{7,71},{8,72},{9,... | collective-permute-start | bytes 1290248 | tf_op jit(solution)/shard_map/ppermute | solution.py:29
  319.3 192.0 %copy-start = (f32[112,960]{1,0:T(8,128)}, f32[112,960]{1,0:T(8,128)S(1)}, u32[]{:S(2)}) copy-start(f32[112,960]{1,0:T(8,128)S(1)} %get-tuple-element.58) | copy-start | bytes 1290244
  364.4 18.9 %copy-start.123 = (pred[112,112]{0,1:T(8,128)(4,1)S(1)}, pred[112,112]{0,1:T(8,128)(4,1)}, u32[]{:S(2)}) copy-start(pred[112,112]{0,1:T(8,128)(4,1)} %get-tuple-element.169) | copy-start | bytes 37636
  393.2 112.1 %copy-start.3 = (f32[112,960]{1,0:T(8,128)}, f32[112,960]{1,0:T(8,128)S(1)}, u32[]{:S(2)}) copy-start(f32[112,960]{1,0:T(8,128)S(1)} %get-tuple-element.156) | copy-start | bytes 1290244
  397.5 16.2 %collective-permute-start.2 = (f32[112,960]{1,0:T(8,128)S(1)}, f32[112,960]{1,0:T(8,128)S(1)}, u32[]{:S(2)}, u32[]{:S(2)}) collective-permute-start(f32[112,960]{1,0:T(8,128)S(1)} %multiply_add_fusion.3), channel_id=1, source_target_pairs={{64,0},{65,1},{66,2},{67,3},{68,4},{69,5},{70,6},{71,7},{72,8},{73... | collective-permute-start | bytes 1290248 | tf_op jit(solution)/shard_map/ppermute | solution.py:29
  398.8 14.9 %slice-start.22 = ((s8[4915200]{0:T(1024)(128)(4,1)}), s8[4194304]{0:T(1024)(128)(4,1)S(1)}, s32[]{:S(2)}) async-start(s8[4915200]{0:T(1024)(128)(4,1)} %bitcast.616), calls=%async_computation.31 | async-start | bytes 8388608
  434.3 15.3 %slice-start = ((s8[9830400]{0:T(1024)(128)(4,1)}), s8[4194304]{0:T(1024)(128)(4,1)S(1)}, s32[]{:S(2)}) async-start(s8[9830400]{0:T(1024)(128)(4,1)} %bitcast.503), calls=%async_computation.9 | async-start | bytes 8388608
  435.3 14.3 %slice-start.1 = ((s8[9830400]{0:T(1024)(128)(4,1)}), s8[4194304]{0:T(1024)(128)(4,1)S(1)}, s32[]{:S(2)}) async-start(s8[9830400]{0:T(1024)(128)(4,1)} %bitcast.503), calls=%async_computation.10 | async-start | bytes 8388608
  435.3 14.3 %slice-start.2 = ((s8[9830400]{0:T(1024)(128)(4,1)}), s8[1441792]{0:T(1024)(128)(4,1)S(1)}, s32[]{:S(2)}) async-start(s8[9830400]{0:T(1024)(128)(4,1)} %bitcast.503), calls=%async_computation.11 | async-start | bytes 2883584
  435.3 14.3 %copy-start.51 = (f32[112,5120]{1,0:T(8,128)S(1)}, f32[112,5120]{1,0:T(8,128)}, u32[]{:S(2)}) copy-start(f32[112,5120]{1,0:T(8,128)} %fusion.89) | copy-start | bytes 6881284
  435.4 12.8 %collective-permute-start.3 = (f32[112,960]{1,0:T(8,128)S(1)}, f32[112,960]{1,0:T(8,128)S(1)}, u32[]{:S(2)}, u32[]{:S(2)}) collective-permute-start(f32[112,960]{1,0:T(8,128)S(1)} %get-tuple-element.56), channel_id=1, source_target_pairs={{64,0},{65,1},{66,2},{67,3},{68,4},{69,5},{70,6},{71,7},{72,8},{73... | collective-permute-start | bytes 1290248 | tf_op jit(solution)/shard_map/ppermute | solution.py:29
  456.0 144.3 %reduce-scatter.20.cloned.1.call-start = ((), (), s32[]{:S(2)}) async-start(), calls=%async_computation.7 | async-start | bytes 368640
  484.2 15.2 %slice-start.24 = ((s8[4915200]{0:T(1024)(128)(4,1)}), s8[4194304]{0:T(1024)(128)(4,1)S(1)}, s32[]{:S(2)}) async-start(s8[4915200]{0:T(1024)(128)(4,1)} %bitcast.618), calls=%async_computation.33 | async-start | bytes 8388608
  517.4 223.9 %reduce-scatter.16.cloned.1.call-start = ((), (), s32[]{:S(2)}) async-start(), calls=%async_computation.5 | async-start | bytes 22118400 | tf_op jit(solution)/shard_map/reduce_scatter | solution.py:34
  523.6 18.3 %copy-start.32 = (bf16[5,64,3,112]{3,1,2,0:T(8,128)(2,1)S(1)}, bf16[5,64,3,112]{3,1,2,0:T(8,128)(2,1)}, u32[]{:S(2)}) copy-start(bf16[5,64,3,112]{3,1,2,0:T(8,128)(2,1)} %copy-done.31) | copy-start | bytes 645124
  568.7 296.3 %all-reduce.11.cloned.1.call-start = ((), (), s32[]{:S(2)}) async-start(), calls=%async_computation.8 | async-start | bytes 10485760
  827.7 51.0 %collective-permute-start.6 = (bf16[16,960]{1,0:T(8,128)(2,1)S(1)}, bf16[16,960]{1,0:T(8,128)(2,1)S(1)}, u32[]{:S(2)}, u32[]{:S(2)}) collective-permute-start(bf16[16,960]{1,0:T(8,128)(2,1)S(1)} %get-tuple-element.53), channel_id=1, source_target_pairs={{0,1},{1,2},{2,3},{3,4},{4,5},{5,6},{6,7},{7,8},{8,9},{9,10},{10,1... | collective-permute-start | bytes 92168
  829.7 47.1 %collective-permute-start.7 = (bf16[15,960]{1,0:T(8,128)(2,1)S(1)}, bf16[15,960]{1,0:T(8,128)(2,1)S(1)}, u32[]{:S(2)}, u32[]{:S(2)}) collective-permute-start(bf16[15,960]{1,0:T(8,128)(2,1)S(1)} %slice.446), channel_id=1, source_target_pairs={{0,2},{1,3},{2,4},{3,5},{4,6},{5,7},{6,8},{7,9},{8,10},{9,11},{10,... | collective-permute-start | bytes 86408
  866.7 13.0 %collective-permute-start.4 = (bf16[16,1600]{1,0:T(8,128)(2,1)S(1)}, bf16[16,1600]{1,0:T(8,128)(2,1)S(1)}, u32[]{:S(2)}, u32[]{:S(2)}) collective-permute-start(bf16[16,1600]{1,0:T(8,128)(2,1)S(1)} %get-tuple-element.52), channel_id=1, source_target_pairs={{0,1},{1,2},{2,3},{3,4},{4,5},{5,6},{6,7},{7,8},{8,9},{9,10},{10,1... | collective-permute-start | bytes 153608
  868.8 15.7 %collective-permute-start.8 = (bf16[16,5120]{1,0:T(8,128)(2,1)S(1)}, bf16[16,5120]{1,0:T(8,128)(2,1)S(1)}, u32[]{:S(2)}, u32[]{:S(2)}) collective-permute-start(bf16[16,5120]{1,0:T(8,128)(2,1)S(1)} %get-tuple-element.54), channel_id=1, source_target_pairs={{0,1},{1,2},{2,3},{3,4},{4,5},{5,6},{6,7},{7,8},{8,9},{9,10},{10,1... | collective-permute-start | bytes 491528
  872.2 7.6 collective-permute-start.5
  876.8 7.7 collective-permute-start.9
  (172 other events, 731.8 us)
Sparse Core Ops, SparseCore 0:
  19.2 182.6 all-gather.2
  203.5 68.3 all-gather.4
  456.1 66.4 reduce-scatter.17
  525.4 14.9 reduce-scatter.19
  568.8 172.4 reduce-scatter.15
  744.5 120.3 all-reduce.10
where the time goes:
time: 899 us; the launch traced here: 894 us
  waiting for transfers between devices  359 us (40%)
  matrix products  209 us (23%)
  blocking collectives  149 us (17%)
  local copies, waits for them, and re-layouts  96.2 us (11%)
  other arithmetic  34.9 us (4%)
  starting transfers between devices  26.6 us (3%)
  between operations  19.2 us (2%)
    all_gather x1, waiting for transfers between devices, sent_together(): result, at, outs = (lax.all_gather(both, axis, axis=dim, tiled=True), 0, [])  164 us
    unnamed x2, blocking collectives  139 us
    reduce_scatter x1, waiting for transfers between devices, side_by_side(): lax.psum_scatter(both, axis, scatter_dimension=dim, tiled=True)  79.6 us
    all_gather x1, waiting for transfers between devices, fetch_weights(): lax.all_gather(down_weight, 'shard', axis=1, tiled=True)  54.4 us
    dot_general x3, matrix products, backward(): jnp.dot(ffn_norm.T, gateup_in, preferred_element_type=jnp.float32)  38 us
    unnamed x14, waiting for transfers between devices  37.7 us
    dot_general x6, matrix products, forward(): gateup = jnp.dot(ffn_norm, gateup_full, preferred_element_type=jnp.float32)  33.5 us
    ppermute x4, waiting for transfers between devices, from_behind(): return lax.ppermute(shard, axis, pairs)  23.2 us
  transfers between devices with their start and end apart: 16, of which 8 were waited for; matrix products, arithmetic and copies ran while one was open for 30% of the time, Pallas kernels for 0%

commit v1 on v0

v1 whole, which is shorter than its diff:
```python
import functools

import jax
import jax.numpy as jnp
import numpy as np
from jax import lax
from jax.experimental import pallas as pl
from jax.experimental.pallas import tpu as pltpu
from jax.sharding import Mesh
from jax.sharding import PartitionSpec as P

D = 960
HEADS = 15
KV_HEADS = 5
GROUP = HEADS // KV_HEADS
HEAD = 64
FF = 2560
QKV = 1600
ROWS = 112
LANES = 128
BLOCKS = 13
EPSILON = 1e-05
ROPE_BASE = 100000.0
NEGATIVE = -1e30
HEAD_SCALE = HEAD ** (-0.5)
BF16 = jnp.bfloat16
F32 = jnp.float32
REP = ("z", "x", "core")
SWAP = [(0, 1), (1, 0)]
VMEM_LIMIT = 48 * 1024 * 1024


def lane_ids(rows):
    return lax.broadcasted_iota(jnp.int32, (rows, LANES), 1)


def swapped_halves(x, low_half):
    return jnp.where(low_half, pltpu.roll(x, LANES - 32, 1), pltpu.roll(x, 32, 1))


def block_of(ref, index, width):
    start = index * LANES
    stop = min(start + LANES, width)
    part = ref[:, start:stop]
    if stop - start < LANES:
        part = jnp.concatenate([part, jnp.zeros((part.shape[0], LANES - (stop - start)), part.dtype)], axis=1)
    return part


def both_halves(block, slot, left):
    if slot == 0:
        low = jnp.where(left, block, 0.0)
        high = pltpu.roll(low, HEAD, 1)
    else:
        high = jnp.where(left, 0.0, block)
        low = pltpu.roll(high, HEAD, 1)
    return low.astype(BF16), high.astype(BF16)


def contract(a, b, dims):
    return lax.dot_general(a, b, ((dims[0:1], dims[1:2]), ((), ())), preferred_element_type=F32)


def attend_kernel(proj_ref, mask_ref, cos_ref, sin_ref, heads_ref, prob_ref, mixed_ref):
    lanes = lane_ids(ROWS)
    left = lanes < HEAD
    low_half = (lanes % HEAD) < 32
    cos = cos_ref[...]
    sin = sin_ref[...]
    mask = mask_ref[0] > 0.0
    blocks = []
    for b in range(BLOCKS):
        x = block_of(proj_ref, b, QKV)
        if b < 10:
            x = x * cos + swapped_halves(x, low_half) * sin
        low = x.astype(BF16)
        blocks.append(low)
        stop = min(b * LANES + LANES, QKV)
        heads_ref[:, b * LANES : stop] = low[:, : stop - b * LANES]
    mixed = [None] * 8
    for kk in range(KV_HEADS):
        kslot, vslot = HEADS + kk, HEADS + KV_HEADS + kk
        keys = both_halves(blocks[kslot // 2].astype(F32), kslot % 2, left)
        values = both_halves(blocks[vslot // 2].astype(F32), vslot % 2, left)
        for h in range(kk * GROUP, kk * GROUP + GROUP):
            half, b = h % 2, h // 2
            scores = contract(keys[half], blocks[b], (1, 1)) * HEAD_SCALE
            scores = jnp.where(mask, scores, NEGATIVE)
            top = jnp.max(scores, axis=0, keepdims=True)
            raised = jnp.exp(scores - top)
            prob = raised / jnp.sum(raised, axis=0, keepdims=True)
            prob_ref[0, h] = prob
            part = contract(prob.astype(BF16), values[half], (0, 0))
            mixed[b] = part if mixed[b] is None else mixed[b] + part
    for b in range(8):
        stop = min(b * LANES + LANES, D)
        mixed_ref[:, b * LANES : stop] = mixed[b].astype(BF16)[:, : stop - b * LANES]


def attend_back_kernel(heads_ref, prob_ref, dmixed_ref, cos_ref, sin_ref, out_ref):
    lanes = lane_ids(ROWS)
    left = lanes < HEAD
    low_half = (lanes % HEAD) < 32
    cos = cos_ref[...]
    sin = sin_ref[...]
    blocks = [block_of(heads_ref, b, QKV) for b in range(BLOCKS)]
    dmixed = [block_of(dmixed_ref, b, D) for b in range(8)]
    outs = [None] * BLOCKS

    def add(index, term):
        outs[index] = term if outs[index] is None else outs[index] + term

    for kk in range(KV_HEADS):
        kslot, vslot = HEADS + kk, HEADS + KV_HEADS + kk
        keys = both_halves(blocks[kslot // 2].astype(F32), kslot % 2, left)
        values = both_halves(blocks[vslot // 2].astype(F32), vslot % 2, left)
        dkeys = [None, None]
        dvalues = [None, None]
        for h in range(kk * GROUP, kk * GROUP + GROUP):
            half, b = h % 2, h // 2
            prob = prob_ref[0, h]
            dprob = contract(values[half], dmixed[b], (1, 1))
            inner = jnp.sum(dprob * prob, axis=0, keepdims=True)
            dscore = (prob * (dprob - inner)).astype(BF16)
            add(b, contract(dscore, keys[half], (0, 0)))
            dk = contract(dscore, blocks[b], (1, 0))
            dv = contract(prob.astype(BF16), dmixed[b], (1, 0))
            dkeys[half] = dk if dkeys[half] is None else dkeys[half] + dk
            dvalues[half] = dv if dvalues[half] is None else dvalues[half] + dv
        for slot, (low, high) in ((kslot, dkeys), (vslot, dvalues)):
            low = jnp.where(left, low, 0.0)
            high = jnp.where(left, 0.0, high)
            if slot % 2 == 0:
                term = low + pltpu.roll(high, HEAD, 1)
            else:
                term = pltpu.roll(low, HEAD, 1) + high
            add(slot // 2, term)
    for b in range(BLOCKS):
        x = outs[b]
        if b < 10:
            x = x * HEAD_SCALE
            x = x * cos - swapped_halves(x, low_half) * sin
        stop = min(b * LANES + LANES, QKV)
        out_ref[:, b * LANES : stop] = x.astype(BF16)[:, : stop - b * LANES]


def row_spec(width):
    return pl.BlockSpec((ROWS, width), lambda i: (i, 0))


def attend(projected, mask, cos, sin):
    count = mask.shape[0]
    rows = count * ROWS
    return pl.pallas_call(
        attend_kernel,
        grid=(count,),
        in_specs=[
            row_spec(QKV),
            pl.BlockSpec((1, ROWS, ROWS), lambda i: (i, 0, 0)),
            row_spec(LANES),
            row_spec(LANES),
        ],
        out_specs=[
            row_spec(QKV),
            pl.BlockSpec((1, HEADS, ROWS, ROWS), lambda i: (i, 0, 0, 0)),
            row_spec(D),
        ],
        out_shape=[
            jax.ShapeDtypeStruct((rows, QKV), BF16),
            jax.ShapeDtypeStruct((count, HEADS, ROWS, ROWS), F32),
            jax.ShapeDtypeStruct((rows, D), BF16),
        ],
        compiler_params=pltpu.CompilerParams(vmem_limit_bytes=VMEM_LIMIT),
        name="attend",
    )(projected, mask, cos, sin)


def attend_back(heads, prob, dmixed, cos, sin):
    count = prob.shape[0]
    rows = count * ROWS
    return pl.pallas_call(
        attend_back_kernel,
        grid=(count,),
        in_specs=[
            row_spec(QKV),
            pl.BlockSpec((1, HEADS, ROWS, ROWS), lambda i: (i, 0, 0, 0)),
            row_spec(D),
            row_spec(LANES),
            row_spec(LANES),
        ],
        out_specs=row_spec(QKV),
        out_shape=jax.ShapeDtypeStruct((rows, QKV), BF16),
        compiler_params=pltpu.CompilerParams(vmem_limit_bytes=VMEM_LIMIT),
        name="attend_back",
    )(heads, prob, dmixed, cos, sin)


def tables(segments):
    count, rows = segments.shape
    earlier = jnp.sum((segments[:, None, :] < segments[:, :, None]).astype(jnp.int32), axis=2)
    position = (jnp.arange(rows, dtype=jnp.int32)[None, :] - earlier).astype(F32).reshape(count * rows, 1)
    frequency = ROPE_BASE ** (-jnp.arange(HEAD // 2, dtype=F32) * 2.0 / HEAD)
    angles = position * frequency[None, :]
    cos, sin = jnp.cos(angles), jnp.sin(angles)
    order = jnp.arange(rows, dtype=jnp.int32)
    mask = (segments[:, :, None] == segments[:, None, :]) & (order[:, None] <= order[None, :])[None]
    return (
        jnp.concatenate([cos] * 4, axis=1),
        jnp.concatenate([-sin, sin, -sin, sin], axis=1),
        mask.astype(F32),
    )


def mm(a, b):
    return jnp.dot(a, b, preferred_element_type=F32)


def mmt(a, b):
    return lax.dot_general(a, b, (((1,), (1,)), ((), ())), preferred_element_type=F32)


def halves(x, first):
    cut = x.shape[1] // 2
    own = jnp.where(first, x[:, :cut], x[:, cut:])
    other = jnp.where(first, x[:, cut:], x[:, :cut])
    if cut == 480:
        other = jnp.pad(other, ((0, 0), (0, 32)))
    return own, other


def times(x, weight, first):
    own, other = halves(x, first)
    return mm(own, weight[0]) + mm(other, weight[1])


def times_back(x, weight, first):
    own, other = mmt(x, weight[0]), mmt(x, weight[1])[:, : weight[0].shape[0]]
    return jnp.concatenate([jnp.where(first, own, other), jnp.where(first, other, own)], axis=1)


def layer_forward(stream, first, gains, weights, table):
    qkv_w, out_w, gateup_w, down_w = weights
    cos, sin, mask = table
    first_scale = lax.rsqrt(jnp.mean(stream * stream, axis=-1, keepdims=True) + EPSILON)
    attn_norm = (stream * first_scale * gains[0]).astype(BF16)
    projected = times(attn_norm, qkv_w, first)
    heads, prob, mixed = attend(projected, mask, cos, sin)
    middle = stream + times(mixed, out_w, first)
    second_scale = lax.rsqrt(jnp.mean(middle * middle, axis=-1, keepdims=True) + EPSILON)
    ffn_norm = (middle * second_scale * gains[1]).astype(BF16)
    gateup = times(ffn_norm, gateup_w, first)
    gate, up = gateup[:, :FF], gateup[:, FF:]
    hidden = (gate * jax.nn.sigmoid(gate) * up).astype(BF16)
    output = middle + times(hidden, down_w, first)
    return output, (stream, first_scale, attn_norm, heads, prob, mixed, middle, second_scale, ffn_norm, gate, up, hidden)


def norm_back(incoming, gain, scale, normed):
    scaled = incoming * gain
    return scale * (scaled - normed * jnp.mean(scaled * normed, axis=-1, keepdims=True))


def layer_backward(dy, kept, first, gains, weights, table, grads):
    qkv_w, out_w, gateup_w, down_w = weights
    cos, sin, _ = table
    stream, first_scale, attn_norm, heads, prob, mixed, middle, second_scale, ffn_norm, gate, up, hidden = kept
    dz = dy.astype(BF16)
    if grads is not None:
        grads.down(hidden, dz)
    dhidden = times_back(dz, down_w, first)
    s = jax.nn.sigmoid(gate)
    dgateup = jnp.concatenate(
        [dhidden * up * s * (1.0 + gate * (1.0 - s)), dhidden * gate * s], axis=1
    ).astype(BF16)
    if grads is not None:
        grads.rows("gateup", ffn_norm, dgateup)
    dffn = times_back(dgateup, gateup_w, first)
    second_normed = middle * second_scale
    dmiddle = dy + norm_back(dffn, gains[1], second_scale, second_normed)
    dbranch = dmiddle.astype(BF16)
    if grads is not None:
        grads.rows("output", mixed, dbranch)
    dmixed = times_back(dbranch, out_w, first).astype(BF16)
    dprojected = attend_back(heads, prob, dmixed, cos, sin)
    dattn = times_back(dprojected, qkv_w, first)
    first_normed = stream * first_scale
    if grads is not None:
        gain_grads = jnp.stack([jnp.sum(dattn * first_normed, axis=0), jnp.sum(dffn * second_normed, axis=0)], axis=1)
        grads.rows("qkv", attn_norm, dprojected, gain_grads)
    return dmiddle + norm_back(dattn, gains[0], first_scale, first_normed)


def row_order():
    pick = np.zeros((D, 1024), np.float32)
    for row in range(D):
        s, rest = divmod(row, 480)
        chunk, i = divmod(rest, 30)
        pick[row, chunk * 64 + s * 32 + i] = 1.0
    return pick


class Gradients:
    def __init__(self):
        self.core = lax.axis_index("core") == 0
        self.shard = lax.axis_index("shard") == 0
        self.pick = jnp.asarray(row_order(), BF16)
        self.found = {}

    def shared(self, left, right):
        cut = right.shape[1] // 2
        keep = jnp.where(self.core, right[:, :cut], right[:, cut:])
        give = jnp.where(self.core, right[:, cut:], right[:, :cut])
        left_other = lax.ppermute(left, "core", SWAP)
        right_other = lax.ppermute(give, "core", SWAP)
        return jnp.concatenate([left, left_other], axis=0), jnp.concatenate([keep, right_other], axis=0)

    def scatter(self, value):
        return lax.psum_scatter(value, ("z", "x"), scatter_dimension=0, tiled=True)

    def joined(self, piece, per_core):
        columns = piece.shape[1]
        parts = piece.reshape(2, 2, per_core, columns)
        by_shard = jnp.where(self.shard, parts, parts[::-1])
        by_both = jnp.where(self.core, by_shard, by_shard[:, ::-1])
        axes = ("shard", "core")
        across = lax.ppermute(by_both[1, 0], axes, [(0, 2), (2, 0), (1, 3), (3, 1)]).astype(F32)
        beside = lax.ppermute(by_both[0, 1], axes, [(0, 1), (1, 0), (2, 3), (3, 2)]).astype(F32)
        corner = lax.ppermute(by_both[1, 1], axes, [(0, 3), (3, 0), (1, 2), (2, 1)]).astype(F32)
        own = by_both[0, 0].astype(F32) + across
        other = beside + corner
        return jnp.where(self.core, own, other), jnp.where(self.core, other, own)

    def down(self, hidden, dz):
        left, right = self.shared(hidden, dz)
        made = [
            lax.dot_general(part, right, (((0,), (0,)), ((), ())), preferred_element_type=F32).astype(BF16)
            for part in (left[:, : FF // 2], left[:, FF // 2 :])
        ]
        whole = jnp.stack([m.reshape(16, 80, 480) for m in made], axis=1).reshape(FF, 480)
        self.found["down"] = jnp.concatenate(self.joined(self.scatter(whole), 40), axis=1)[None]

    def rows(self, name, left, right, extra=None):
        picked = mm(left, self.pick).astype(BF16)
        left, right = self.shared(picked, right)
        whole = lax.dot_general(left, right, (((0,), (0,)), ((), ())), preferred_element_type=F32).astype(BF16)
        width = whole.shape[1]
        if extra is not None:
            extra = lax.dot_general(self.pick, extra.astype(BF16), (((0,), (0,)), ((), ())), preferred_element_type=F32)
            whole = jnp.concatenate([whole, extra.astype(BF16)], axis=1)
        piece = self.scatter(whole)
        piece = piece.reshape(2, 32, piece.shape[1])[:, :30].reshape(60, piece.shape[1])
        low, high = self.joined(piece, 15)
        self.found[name] = jnp.concatenate([low[:, :width], high[:, :width]], axis=1)[None]
        if extra is not None:
            self.found["gains"] = (low[:, width:] + high[:, width:]).T[None]


def shards(tokens, segments, cotangent, qkv_weight, output_weight, gateup_weight, down_weight, norm_gains):
    leading = lax.axis_index("section") == 0
    first = lax.axis_index("shard") == 0
    rep = lax.axis_index(REP)

    owned = (qkv_weight[0], output_weight[0], gateup_weight[0])
    start = jnp.minimum(rep * 16, 464)
    slices = jnp.concatenate([lax.dynamic_slice_in_dim(w, start, 16, 0) for w in owned], axis=1)
    slices = lax.ppermute(slices, "shard", SWAP)
    down_slice = lax.ppermute(lax.dynamic_slice_in_dim(down_weight[0], rep * 40, 40, 0), "shard", SWAP)
    other_gains = lax.ppermute(norm_gains[0], "shard", SWAP)
    own_gains = norm_gains[0]
    gains = jnp.concatenate(
        [jnp.where(first, own_gains, other_gains), jnp.where(first, other_gains, own_gains)], axis=1
    ).astype(F32)
    weights, at = [], 0
    for w in owned:
        piece = slices[:, at : at + w.shape[1]]
        at += w.shape[1]
        weights.append((w, lax.all_gather(piece, REP, axis=0, tiled=True)))
    weights.append((down_weight[0], lax.all_gather(down_slice, REP, axis=0, tiled=True)))

    table = tables(segments)
    inputs = tokens.astype(F32)
    early, _ = layer_forward(inputs, first, gains, weights, table)
    arrived = lax.ppermute(early.astype(BF16), "section", [(0, 1)]).astype(F32)
    stream = jnp.where(leading, inputs, arrived)
    output, kept = layer_forward(stream, first, gains, weights, table)

    early = layer_backward(cotangent, kept, first, gains, weights, table, None)
    arrived = lax.ppermute(early.astype(BF16), "section", [(1, 0)]).astype(F32)
    dy = jnp.where(leading, arrived, cotangent)
    grads = Gradients()
    down = layer_backward(dy, kept, first, gains, weights, table, grads)
    found = grads.found
    return (
        output[None],
        down[None],
        found["qkv"],
        found["output"],
        found["gateup"],
        found["down"],
        found["gains"],
    )


def solution(mesh):
    sizes = mesh.shape
    fine = Mesh(
        mesh.devices.reshape(sizes["section"], sizes["shard"], 4, 4, 2),
        ("section", "shard", "z", "x", "core"),
    )
    tokens = ("shard",) + REP
    in_specs = (
        P(tokens, None),
        P(tokens, None),
        P(tokens, None),
        P("section", "shard", None),
        P("section", "shard", None),
        P("section", "shard", None),
        P("section", "shard", None),
        P("section", None, "shard"),
    )
    out_specs = (
        P("section", tokens, None),
        P("section", tokens, None),
        P("section", tokens, None),
        P("section", tokens, None),
        P("section", tokens, None),
        P("section", tokens, None),
        P("section", None, tokens),
    )
    return jax.shard_map(shards, mesh=fine, in_specs=in_specs, out_specs=out_specs, check_vma=False)
```

time: 899 us -> 581 us (0.65)
  matrix products: 209 us -> 76.8 us
  blocking collectives: 149 us -> 28.5 us
  local copies, waits for them, and re-layouts: 96.2 us -> 35.6 us
  waiting for transfers between devices: 359 us -> 341 us
  Pallas kernels: 0 us -> 16.9 us
    reduce_scatter x2 -> x4, waiting for transfers between devices: 79.7 us -> 224 us  [scatter(): return lax.psum_scatter(value, ('z', 'x'), scatter_dimension=0, tiled=True)]
    all_gather x2 -> x3, waiting for transfers between devices: 218 us -> 75.9 us  [the longest x2 38.5 us: shards(): weights.append((w, lax.all_gather(piece, REP, axis=0, tiled=True)))]
    unnamed x2 -> x0, blocking collectives: 139 us -> none
    dot_general x66 -> x41, matrix products: 203 us -> 76.8 us  [the longest x19 40.3 us: mm(): return jnp.dot(a, b, preferred_element_type=F32)]
    unnamed x14 -> x7, waiting for transfers between devices: 37.7 us -> 0.12 us
    concatenate x2 -> x1, local copies, waits for them, and re-layouts: 33.1 us -> 0.79 us  [shards(): jnp.concatenate([lax.dynamic_slice_in_dim(w, start, 16, 0) for w in owned...]
    slice x42 -> x5, local copies, waits for them, and re-layouts: 27.8 us -> 3.18 us  [the longest x3 2.19 us: shards(): piece = slices[:, at:at + w.shape[1]]]
    ppermute x4 -> x25, starting transfers between devices: 10.4 us -> 29.3 us  [the longest x4 9.94 us: joined(): lax.ppermute(by_both[0, 1], axes, [(0, 1), (1, 0), (2, 3), (3, 2)])]
  transfers between devices with their start and end apart: 16 -> 32, of which waited for: 8 -> 21; matrix products, arithmetic and copies ran while one was open for 30% -> 17% of each run, Pallas kernels for 0% -> 2%
where the time goes in v1:
time: 581 us; the launch traced here: 571 us
  waiting for transfers between devices  341 us (59%)
  matrix products  76.8 us (13%)
  local copies, waits for them, and re-layouts  35.6 us (6%)
  starting transfers between devices  29.6 us (5%)
  blocking collectives  28.5 us (5%)
  other arithmetic  26.9 us (5%)
  Pallas kernels  16.9 us (3%)
  between operations  15.9 us (3%)
    reduce_scatter x4, waiting for transfers between devices, scatter(): return lax.psum_scatter(value, ('z', 'x'), scatter_dimension=0, tiled=True)  224 us
    dot_general x19, matrix products, mm(): return jnp.dot(a, b, preferred_element_type=F32)  40.3 us
    all_gather x2, waiting for transfers between devices, shards(): weights.append((w, lax.all_gather(piece, REP, axis=0, tiled=True)))  38.5 us
    all_gather x1, waiting for transfers between devices, shards(): lax.all_gather(down_slice, REP, axis=0, tiled=True)  37.4 us
    all_gather x1, blocking collectives, shards(): weights.append((w, lax.all_gather(piece, REP, axis=0, tiled=True)))  28.5 us
    dot_general x16, matrix products, mmt(): lax.dot_general(a, b, (((1,), (1,)), ((), ())), preferred_element_type=F32)  20.8 us
    unnamed x149, local copies, waits for them, and re-layouts  17.5 us
    ppermute x4, waiting for transfers between devices, joined(): lax.ppermute(by_both[1, 0], axes, [(0, 2), (2, 0), (1, 3), (3, 1)])  11.9 us
  transfers between devices with their start and end apart: 32, of which 21 were waited for; matrix products, arithmetic and copies ran while one was open for 17% of the time, Pallas kernels for 2%

profile of v1, /device:TPU:2, one launch (start us, length us, event | category | flops | bytes accessed | tf_op | source)
XLA Modules:
  0.0 571.2 jit_solution(808288061896889617)
XLA Ops:
  11.0 3.2 collective-permute-start.1
  14.1 6.2 %collective-permute-done.1 = bf16[16,7680]{1,0:T(8,128)(2,1)S(1)} collective-permute-done((bf16[16,7680]{1,0:T(8,128)(2,1)}, bf16[16,7680]{1,0:T(8,128)(2,1)S(1)}, u32[]{:S(2)}, u32[]{:S(2)}) %collective-permute-start.1) | collective-permute-done | bytes 245792 | tf_op jit(solution)/shard_map/ppermute | solution.py:366
  21.9 3.3 collective-permute-start
  28.8 3.5 collective-permute-done.2
  33.6 3.4 fusion.30
  37.8 28.5 %all_gather.13 = bf16[512,960]{1,0:T(8,128)(2,1)} all-gather(bf16[16,960]{1,0:T(8,128)(2,1)S(1)} %slice.296), channel_id=1, replica_groups=mesh['section'=2,'shard'=2,'z'=4,'x'=4,'core'=2] {'z','x','core'}, dimensions={0}, use_global_device_ids=true | all-gather | bytes 1013760 | tf_op jit(solution)/shard_map/all_gather | solution.py:377
  69.9 3.0 attend.2
  75.6 3.6 fusion.6
  79.2 37.5 %all-gather.6.cloned.1.call-done = bf16[512,5120]{1,0:T(8,128)(2,1)} async-done(((bf16[16,5120]{1,0:T(8,128)(2,1)}), bf16[512,5120]{1,0:T(8,128)(2,1)}) %all-gather.6.cloned.1.call-update) | async-done | bytes 5242896 | tf_op jit(solution)/shard_map/all_gather | solution.py:377
  116.6 5.2 convolution_add_fusion.1
  125.4 37.4 %all-gather.8.cloned.1.call-done = bf16[1280,960]{1,0:T(8,128)(2,1)} async-done(((bf16[40,960]{1,0:T(8,128)(2,1)}), bf16[1280,960]{1,0:T(8,128)(2,1)}) %all-gather.8.cloned.1.call-update) | async-done | bytes 2457616 | tf_op jit(solution)/shard_map/all_gather | solution.py:378
  162.8 4.3 fusion.40
  167.1 3.8 collective-permute-start.3
  172.7 4.8 broadcast_select_fusion.7
  177.5 3.5 collective-permute-done.3
  187.2 4.2 fusion.4
  191.6 4.0 convolution_add_fusion
  204.0 5.9 %attend_back.2 = bf16[224,1600]{1,0:T(8,128)(2,1)S(1)} custom-call(bf16[224,1600]{1,0:T(8,128)(2,1)S(1)} %get-tuple-element.13.heads_ref, f32[2,15,112,112]{3,2,1,0:T(8,128)S(1)} %get-tuple-element.14.prob_ref, bf16[224,960]{1,0:T(8,128)(2,1)S(1)} %pad_maximum_fusion.14.dmixed_ref, f32[224,128]{1,0:T(8,128)S(1)} %get-tuple-element.125.cos_ref, ...), custom_call_target="tpu_custom_call" | custom-call | tf_op jit(solution)/shard_map/attend_back/pallas_call | solution.py:181
  216.5 9.8 %collective-permute-done.4 = bf16[224,960]{1,0:T(8,128)(2,1)S(1)} collective-permute-done((bf16[224,960]{1,0:T(8,128)(2,1)S(1)}, bf16[224,960]{1,0:T(8,128)(2,1)S(1)}, u32[]{:S(2)}, u32[]{:S(2)}) %collective-permute-start.4) | collective-permute-done | bytes 430112 | tf_op jit(solution)/shard_map/ppermute | solution.py:388
  242.4 5.9 %attend_back.3 = bf16[224,1600]{1,0:T(8,128)(2,1)S(1)} custom-call(bf16[224,1600]{1,0:T(8,128)(2,1)S(1)} %get-tuple-element.13.heads_ref, f32[2,15,112,112]{3,2,1,0:T(8,128)S(1)} %copy-done.2, bf16[224,960]{1,0:T(8,128)(2,1)S(1)} %pad_maximum_fusion.15.dmixed_ref, f32[224,128]{1,0:T(8,128)S(1)} %get-tuple-element.125.cos_ref, ...), custom_call_target="tpu_custom_call" | custom-call | tf_op jit(solution)/shard_map/attend_back/pallas_call | solution.py:181
  255.9 3.7 copy.105
  264.0 3.0 convolution_convert_fusion.1
  269.4 3.3 convolution_convert_fusion.2
  284.1 5.1 convolution_convert_fusion
  291.5 3.0 fusion.37
  294.5 17.8 %reduce-scatter.7.cloned.1.call-done = bf16[64,480]{1,0:T(8,128)(2,1)} async-done(((bf16[1024,480]{1,0:T(8,128)(2,1)}), bf16[64,480]{1,0:T(8,128)(2,1)}) %reduce-scatter.7.cloned.1.call-update) | async-done | bytes 61456 | tf_op jit(solution)/shard_map/reduce_scatter | solution.py:318
  322.4 66.7 %reduce-scatter.13.cloned.1.call-done = bf16[64,802]{1,0:T(8,128)(2,1)} async-done(((bf16[1024,802]{1,0:T(8,128)(2,1)}), bf16[64,802]{1,0:T(8,128)(2,1)}) %reduce-scatter.13.cloned.1.call-update) | async-done | bytes 102672 | tf_op jit(solution)/shard_map/reduce_scatter | solution.py:318
  396.2 3.5 collective-permute-done.7
  399.8 67.3 %reduce-scatter.11.cloned.1.call-done = bf16[160,480]{1,0:T(8,128)(2,1)} async-done(((bf16[2560,480]{1,0:T(8,128)(2,1)}), bf16[160,480]{1,0:T(8,128)(2,1)}) %reduce-scatter.11.cloned.1.call-update) | async-done | bytes 153616 | tf_op jit(solution)/shard_map/reduce_scatter | solution.py:318
  473.6 3.3 collective-permute-done.22
  477.0 72.3 %reduce-scatter.9.cloned.1.call-done = bf16[64,2560]{1,0:T(8,128)(2,1)} async-done(((bf16[1024,2560]{1,0:T(8,128)(2,1)}), bf16[64,2560]{1,0:T(8,128)(2,1)}) %reduce-scatter.9.cloned.1.call-update) | async-done | bytes 327696 | tf_op jit(solution)/shard_map/reduce_scatter | solution.py:318
  559.7 3.1 collective-permute-done.17
  (330 shorter events, 122.3 us)
Async XLA Ops:
  7.2 60.1 %all-gather.4.cloned.1.call-start = ((), (), s32[]{:S(2)}) async-start(), calls=%async_computation.4 | async-start | bytes 1757184 | tf_op jit(solution)/shard_map/all_gather | solution.py:377
  11.0 9.4 %collective-permute-start.1 = (bf16[16,7680]{1,0:T(8,128)(2,1)}, bf16[16,7680]{1,0:T(8,128)(2,1)S(1)}, u32[]{:S(2)}, u32[]{:S(2)}) collective-permute-start(bf16[16,7680]{1,0:T(8,128)(2,1)} %concatenate.86), channel_id=1, source_target_pairs={{0,32},{32,0},{1,33},{33,1},{2,34},{34,2},{3,35},{35,3},{4,36},{36... | collective-permute-start | bytes 737288 | tf_op jit(solution)/shard_map/ppermute | solution.py:366
  21.1 95.6 %all-gather.6.cloned.1.call-start = ((), (), s32[]{:S(2)}) async-start(), calls=%async_computation.5 | async-start | bytes 5406720 | tf_op jit(solution)/shard_map/all_gather | solution.py:377
  21.8 141.0 %all-gather.8.cloned.1.call-start = ((), (), s32[]{:S(2)}) async-start(), calls=%async_computation.6 | async-start | bytes 2703360 | tf_op jit(solution)/shard_map/all_gather | solution.py:378
  21.9 5.9 %collective-permute-start = (bf16[2,480]{1,0:T(2,128)(2,1)}, bf16[2,480]{1,0:T(2,128)(2,1)S(1)}, u32[]{:S(2)}, u32[]{:S(2)}) collective-permute-start(bf16[2,480]{1,0:T(2,128)(2,1)} %bitcast.216), channel_id=1, source_target_pairs={{0,32},{32,0},{1,33},{33,1},{2,34},{34,2},{3,35},{35,3},{4,36},{36... | collective-permute-start | bytes 5768 | tf_op jit(solution)/shard_map/ppermute | solution.py:368
  26.0 6.3 %collective-permute-start.2 = (bf16[40,960]{1,0:T(8,128)(2,1)}, bf16[40,960]{1,0:T(8,128)(2,1)}, u32[]{:S(2)}, u32[]{:S(2)}) collective-permute-start(bf16[40,960]{1,0:T(8,128)(2,1)} %bitcast.10), channel_id=1, source_target_pairs={{0,32},{32,0},{1,33},{33,1},{2,34},{34,2},{3,35},{35,3},{4,36},{36... | collective-permute-start | bytes 230408 | tf_op jit(solution)/shard_map/ppermute | solution.py:367
  32.3 280.0 %reduce-scatter.7.cloned.1.call-start = ((), (), s32[]{:S(2)}) async-start(), calls=%async_computation.7 | async-start | bytes 1114112 | tf_op jit(solution)/shard_map/reduce_scatter | solution.py:318
  167.1 13.9 %collective-permute-start.3 = (bf16[224,960]{1,0:T(8,128)(2,1)}, bf16[224,960]{1,0:T(8,128)(2,1)S(1)}, u32[]{:S(2)}, u32[]{:S(2)}) collective-permute-start(bf16[224,960]{1,0:T(8,128)(2,1)} %fusion.40), channel_id=1, source_target_pairs={{0,64},{1,65},{2,66},{3,67},{4,68},{5,69},{6,70},{7,71},{8,72},{9,... | collective-permute-start | bytes 1290248 | tf_op jit(solution)/shard_map/ppermute | solution.py:383
  212.4 13.9 %collective-permute-start.4 = (bf16[224,960]{1,0:T(8,128)(2,1)S(1)}, bf16[224,960]{1,0:T(8,128)(2,1)S(1)}, u32[]{:S(2)}, u32[]{:S(2)}) collective-permute-start(bf16[224,960]{1,0:T(8,128)(2,1)S(1)} %add_convert_fusion), channel_id=1, source_target_pairs={{64,0},{65,1},{66,2},{67,3},{68,4},{69,5},{70,6},{71,7},{72,8},{73... | collective-permute-start | bytes 1290248 | tf_op jit(solution)/shard_map/ppermute | solution.py:388
  215.3 37.1 %collective-permute-start.5 = (bf16[224,1024]{1,0:T(8,128)(2,1)}, bf16[224,1024]{1,0:T(8,128)(2,1)}, u32[]{:S(2)}, u32[]{:S(2)}) collective-permute-start(bf16[224,1024]{1,0:T(8,128)(2,1)} %convolution_convert_fusion.7), channel_id=1, source_target_pairs={{0,1},{1,0},{2,3},{3,2},{4,5},{5,4},{6,7},{7,6},{8,9},{9,8},{10,11... | collective-permute-start | bytes 1376264 | tf_op jit(solution)/shard_map/ppermute | solution.py:313
  215.9 22.2 %collective-permute-start.10 = (bf16[224,1024]{1,0:T(8,128)(2,1)S(1)}, bf16[224,1024]{1,0:T(8,128)(2,1)S(1)}, u32[]{:S(2)}, u32[]{:S(2)}) collective-permute-start(bf16[224,1024]{1,0:T(8,128)(2,1)S(1)} %convolution_convert_fusion.6), channel_id=1, source_target_pairs={{0,1},{1,0},{2,3},{3,2},{4,5},{5,4},{6,7},{7,6},{8,9},{9,8},{10,11... | collective-permute-start | bytes 1376264 | tf_op jit(solution)/shard_map/ppermute | solution.py:313
  236.8 1.6 collective-permute-start.11
  240.2 148.9 %reduce-scatter.13.cloned.1.call-start = ((), (), s32[]{:S(2)}) async-start(), calls=%async_computation.10 | async-start | bytes 1949696 | tf_op jit(solution)/shard_map/reduce_scatter | solution.py:318
  248.5 3.8 collective-permute-start.6
  259.7 207.4 %reduce-scatter.11.cloned.1.call-start = ((), (), s32[]{:S(2)}) async-start(), calls=%async_computation.9 | async-start | bytes 2785280 | tf_op jit(solution)/shard_map/reduce_scatter | solution.py:318
  259.7 3.2 collective-permute-start.20
  261.3 1.7 collective-permute-start.21
  278.9 270.3 %reduce-scatter.9.cloned.1.call-start = ((), (), s32[]{:S(2)}) async-start(), calls=%async_computation.8 | async-start | bytes 5570560 | tf_op jit(solution)/shard_map/reduce_scatter | solution.py:318
  280.5 3.5 collective-permute-start.16
  281.7 2.4 collective-permute-start.15
  313.9 6.5 %collective-permute-start.14 = (bf16[15,480]{1,0:T(8,128)(2,1)S(1)}, bf16[15,480]{1,0:T(8,128)(2,1)S(1)}, u32[]{:S(2)}, u32[]{:S(2)}) collective-permute-start(bf16[15,480]{1,0:T(8,128)(2,1)S(1)} %bitcast.213), channel_id=1, source_target_pairs={{0,33},{33,0},{1,32},{32,1},{2,35},{35,2},{3,34},{34,3},{4,37},{37... | collective-permute-start | bytes 43208 | tf_op jit(solution)/shard_map/ppermute | solution.py:328
  314.4 5.9 %collective-permute-start.13 = (bf16[15,480]{1,0:T(8,128)(2,1)S(1)}, bf16[15,480]{1,0:T(8,128)(2,1)S(1)}, u32[]{:S(2)}, u32[]{:S(2)}) collective-permute-start(bf16[15,480]{1,0:T(8,128)(2,1)S(1)} %bitcast.214), channel_id=1, source_target_pairs={{0,1},{1,0},{32,33},{33,32},{2,3},{3,2},{34,35},{35,34},{4,5},{5,4... | collective-permute-start | bytes 43208 | tf_op jit(solution)/shard_map/ppermute | solution.py:327
  317.1 5.2 collective-permute-start.12
  391.1 5.1 collective-permute-start.9
  391.7 4.6 collective-permute-start.8
  394.4 5.4 collective-permute-start.7
  468.2 5.4 collective-permute-start.24
  468.8 4.8 collective-permute-start.23
  471.4 5.5 collective-permute-start.22
  553.5 6.3 %collective-permute-start.19 = (bf16[15,2560]{1,0:T(8,128)(2,1)S(1)}, bf16[15,2560]{1,0:T(8,128)(2,1)S(1)}, u32[]{:S(2)}, u32[]{:S(2)}) collective-permute-start(bf16[15,2560]{1,0:T(8,128)(2,1)S(1)} %bitcast.206), channel_id=1, source_target_pairs={{0,33},{33,0},{1,32},{32,1},{2,35},{35,2},{3,34},{34,3},{4,37},{37... | collective-permute-start | bytes 230408 | tf_op jit(solution)/shard_map/ppermute | solution.py:328
  554.9 4.9 collective-permute-start.18
  556.8 6.0 %collective-permute-start.17 = (bf16[15,2560]{1,0:T(8,128)(2,1)S(1)}, bf16[15,2560]{1,0:T(8,128)(2,1)S(1)}, u32[]{:S(2)}, u32[]{:S(2)}) collective-permute-start(bf16[15,2560]{1,0:T(8,128)(2,1)S(1)} %bitcast.208), channel_id=1, source_target_pairs={{0,32},{32,0},{1,33},{33,1},{2,34},{34,2},{3,35},{35,3},{4,36},{36... | collective-permute-start | bytes 230408 | tf_op jit(solution)/shard_map/ppermute | solution.py:326
  (67 other events, 364.8 us)
Sparse Core Ops, SparseCore 0:
  21.2 46.0 all-gather.3
  70.1 46.4 all-gather.5
  118.9 43.8 all-gather.7
  240.3 71.9 reduce-scatter.6
  315.8 73.2 reduce-scatter.12
  392.6 74.5 reduce-scatter.10
  470.9 78.3 reduce-scatter.8
